TPU v7x, 128 devices: a whole 4x4x4 slice. The times are simulated.
128 devices in a mesh: band: 16 (over x, z_lo, core), pair: 8 (over y, z_hi).
Axes of the slice: x: 4, y: 4, z: 4 (z_hi: 2, z_lo: 2; z = z_hi * 2 + z_lo), core: 2. Of those that a mesh axis runs over, the one named last changes fastest.
Arguments:
- orbitals: float32 [96, 64, 64, 128], P('band'), may hold values from -0.8 to 0.8
Outputs:
- exchange_terms: float32 [96, 64, 64, 128], P('band', 'pair')
All inputs are finite; a program needn't handle non-finite values.
Results may differ from a plain program's by a relative error of at most 0.0003.
Values sent between devices are 32-bit elements; how exact they have to be, the bound alone decides.
A program may use at most 128 MiB of HBM per device.

v0:
```python
import math

import jax
import jax.numpy as jnp
import numpy as np
from jax import lax
from jax.sharding import PartitionSpec as P

grid_spacing = 0.6
screening = 0.106


def passed_along(block, axis, distance):
    devices = range(lax.axis_size(axis))
    route = [((i - distance) % len(devices), i) for i in devices]
    return lax.ppermute(block, axis, route)


def signed_freq(count):
    steps = jnp.arange(count, dtype=jnp.int32)
    signed = jnp.where(steps <= count // 2, steps, steps - count)
    return signed.astype(jnp.float32) * (2.0 * math.pi / (count * grid_spacing))


def screened_kernel(size_x, size_y, size_z):
    fx = signed_freq(size_x)
    fy = signed_freq(size_y)
    fz = signed_freq(size_z)
    square = fx[:, None, None] ** 2 + fy[None, :, None] ** 2 + fz[None, None, :] ** 2
    safe = jnp.where(square > 0, square, jnp.ones_like(square))
    value = 4.0 * math.pi / safe * -jnp.expm1(-safe / (4.0 * screening * screening))
    return jnp.where(square > 0, value, jnp.full_like(value, math.pi / (screening * screening)))


def dft_tables(count):
    steps = jnp.arange(count, dtype=jnp.int32)
    product = steps[:, None] * steps[None, :] % count
    angles = product.astype(jnp.float32) * (2.0 * math.pi / count)
    return (jnp.cos(angles), jnp.sin(angles))


def contract(form, field, table):
    return jnp.einsum(form, field, table, precision=lax.Precision.HIGHEST)


def complex_section(real_part, imag_part, tables, form, sign):
    cosine, sine = tables
    new_real = contract(form, real_part, cosine) - sign * contract(form, imag_part, sine)
    new_imag = contract(form, imag_part, cosine) + sign * contract(form, real_part, sine)
    return (new_real, new_imag)


def poisson(density, kernel, tables_x, tables_y, tables_z):
    real_part = contract("xyz,zk->xyk", density, tables_z[0])
    imag_part = -contract("xyz,zk->xyk", density, tables_z[1])
    real_part, imag_part = complex_section(real_part, imag_part, tables_y, "xyk,yq->xqk", -1.0)
    real_part, imag_part = complex_section(real_part, imag_part, tables_x, "xqk,xp->pqk", -1.0)
    real_part = real_part * kernel
    imag_part = imag_part * kernel
    real_part, imag_part = complex_section(real_part, imag_part, tables_x, "pqk,px->xqk", 1.0)
    real_part, imag_part = complex_section(real_part, imag_part, tables_y, "xqk,qy->xyk", 1.0)
    result = contract("xyk,kz->xyz", real_part, tables_z[0]) - contract(
        "xyk,kz->xyz", imag_part, tables_z[1]
    )
    return result / float(density.shape[0] * density.shape[1] * density.shape[2])


def pair_list(count, pair_count):
    listed = [(first, second, 0, 1) for first in range(count) for second in range(first, count)]
    listed += [(first, second, 1, 1) for first in range(count) for second in range(count)]
    per_device = (len(listed) + pair_count - 1) // pair_count
    listed += [(0, 0, 0, 0)] * (per_device * pair_count - len(listed))
    return (np.array(listed, dtype=np.int32), per_device)


def body(orbitals):
    orbital_count, size_x, size_y, size_z = orbitals.shape
    pair_count = lax.axis_size("pair")
    partner = passed_along(orbitals, "band", -1)
    listed, per_device = pair_list(orbital_count, pair_count)
    layout = listed.reshape(pair_count, per_device, 4)
    rows = jnp.asarray(layout)[lax.axis_index("pair")]
    kernel = screened_kernel(size_x, size_y, size_z)
    tables_x = dft_tables(size_x)
    tables_y = dft_tables(size_y)
    tables_z = dft_tables(size_z)

    def step(counter, carry):
        local_terms, next_terms = carry
        entries = rows[counter]
        first, second, kind = (entries[0], entries[1], entries[2])
        weight = entries[3].astype(jnp.float32)
        orbital_a = lax.dynamic_index_in_dim(orbitals, first, 0, keepdims=False)
        orbital_b = jnp.where(
            kind == 1,
            lax.dynamic_index_in_dim(partner, second, 0, keepdims=False),
            jnp.where(
                kind == 2,
                lax.dynamic_index_in_dim(orbitals, second, 0, keepdims=False),
                lax.dynamic_index_in_dim(orbitals, second, 0, keepdims=False),
            ),
        )
        potential = poisson(orbital_a * orbital_b, kernel, tables_x, tables_y, tables_z)
        local_terms = local_terms.at[first].add(-weight * orbital_b * potential)
        mirrored = -weight * orbital_a * potential
        same_flag = jnp.logical_and(kind == 0, first != second).astype(jnp.float32)
        local_terms = local_terms.at[second].add(same_flag * mirrored)
        cycle_flag = (kind == 1).astype(jnp.float32)
        next_terms = next_terms.at[second].add(cycle_flag * mirrored)
        return (local_terms, next_terms)

    empty = jnp.zeros_like(orbitals)
    local_terms, next_terms = lax.fori_loop(0, per_device, step, (empty, empty))
    total = local_terms + passed_along(next_terms, "band", 1)
    return lax.psum_scatter(total, "pair", scatter_dimension=1, tiled=True)


def solution(mesh):
    return jax.shard_map(
        body,
        mesh=mesh,
        in_specs=(P("band", None, None, None),),
        out_specs=P("band", "pair", None, None),
        check_vma=False,
    )
```

profile of v0, /device:TPU:6, one launch (start us, length us, event | category | flops | bytes accessed | tf_op | source)
XLA Modules:
  0.0 1153.5 jit_solution(3855407082477420192)
XLA Ops:
  8.9 135.4 %collective-permute-done = f32[6,64,64,128]{3,2,1,0:T(8,128)} collective-permute-done((f32[6,64,64,128]{3,2,1,0:T(8,128)}, f32[6,64,64,128]{3,2,1,0:T(8,128)}, u32[]{:S(2)}, u32[]{:S(2)}) %collective-permute-start) | collective-permute-done | bytes 12582944 | tf_op jit(solution)/shard_map/ppermute | solution.py:16
  144.4 6.2 broadcast_in_dim.8.clone
  150.6 6.1 broadcast_in_dim.8
  156.7 654.3 %while.21 = (s32[]{:T(128)}, f32[6,64,64,128]{3,2,1,0:T(8,128)}, f32[6,64,64,128]{3,2,1,0:T(8,128)}, s32[8,4]{0,1:T(4,128)S(1)}, f32[6,64,64,128]{3,2,1,0:T(8,12...) while((s32[]{:T(128)}, f32[6,64,64,128]{3,2,1,0:T(8,128)}, ...), condition=%wide.region_3.4_spmd.clone.clone, body=%wide.region_0.3_spmd.clone.clone.sunk | while | flops 9692250112 | bytes 132159360 | solution.py:113
  168.3 3.7 fusion.308
  188.2 4.4 bitcast_multiply_fusion.7
  196.1 4.4 bitcast_multiply_fusion.6
  225.2 5.7 fusion.319
  230.9 6.7 fusion.320
  269.1 4.4 bitcast_multiply_fusion.7
  277.0 4.4 bitcast_multiply_fusion.6
  300.3 3.7 fusion.313
  306.1 5.7 fusion.319
  311.8 6.7 fusion.320
  349.8 4.4 bitcast_multiply_fusion.7
  354.1 3.7 fusion.309
  357.8 4.4 bitcast_multiply_fusion.6
  386.7 5.7 fusion.319
  392.4 6.8 fusion.320
  410.8 3.7 fusion.308
  430.7 4.4 bitcast_multiply_fusion.7
  438.6 4.4 bitcast_multiply_fusion.6
  467.7 5.7 fusion.319
  473.3 6.7 fusion.320
  511.6 4.4 bitcast_multiply_fusion.7
  519.5 4.4 bitcast_multiply_fusion.6
  542.7 3.7 fusion.313
  548.6 5.7 fusion.319
  554.2 6.7 fusion.320
  592.3 4.4 bitcast_multiply_fusion.7
  596.6 3.7 fusion.309
  600.3 4.4 bitcast_multiply_fusion.6
  629.2 5.7 fusion.319
  634.9 6.7 fusion.320
  673.1 4.4 bitcast_multiply_fusion.7
  681.0 4.4 bitcast_multiply_fusion.6
  710.1 5.6 fusion.319
  715.7 6.7 fusion.320
  753.9 4.4 bitcast_multiply_fusion.7
  761.7 4.4 bitcast_multiply_fusion.6
  785.0 3.7 fusion.313
  790.8 5.6 fusion.319
  796.5 6.8 fusion.320
  811.6 138.5 %collective-permute-done.1 = f32[6,64,64,128]{3,2,1,0:T(8,128)S(1)} collective-permute-done((f32[6,64,64,128]{3,2,1,0:T(8,128)}, f32[6,64,64,128]{3,2,1,0:T(8,128)S(1)}, u32[]{:S(2)}, u32[]{:S(2)}) %collective-permute-start.1) | collective-permute-done | bytes 12582944 | tf_op jit(solution)/shard_map/ppermute | solution.py:16
  950.2 11.1 add.253
  961.3 11.8 %copy.13 = f32[6,64,64,128]{3,2,0,1:T(8,128)} copy(f32[6,64,64,128]{3,2,1,0:T(8,128)} %add.253) | data formatting | bytes 25165824
  973.1 16.2 %copy.39 = f32[8,8,384,128]{3,1,2,0:T(8,128)} copy(f32[8,8,384,128]{3,2,1,0:T(8,128)} %bitcast.214) | data formatting | bytes 25165824
  989.4 154.3 %reduce-scatter.5.cloned.1.call-done = f32[8,49152]{1,0:T(8,128)} async-done(((f32[64,49152]{1,0:T(8,128)}), f32[8,49152]{1,0:T(8,128)}) %reduce-scatter.5.cloned.1.call-update) | async-done | bytes 1572880
  (172 shorter events, 397.3 us)
Async XLA Ops:
  6.5 1137.1 %reduce-scatter.5.cloned.1.call-start = ((), (), s32[]{:S(2)}) async-start(), calls=%async_computation.1 | async-start | bytes 14155776
  6.5 137.8 %collective-permute-start = (f32[6,64,64,128]{3,2,1,0:T(8,128)}, f32[6,64,64,128]{3,2,1,0:T(8,128)}, u32[]{:S(2)}, u32[]{:S(2)}) collective-permute-start(f32[6,64,64,128]{3,2,1,0:T(8,128)} %param.10), channel_id=1, source_target_pairs={{8,0},{16,8},{24,16},{32,24},{40,32},{48,40},{56,48},{64,56},{72,6... | collective-permute-start | bytes 37748744 | tf_op jit(solution)/shard_map/ppermute | solution.py:16
  150.6 6.1 copy-start
  811.0 139.2 %collective-permute-start.1 = (f32[6,64,64,128]{3,2,1,0:T(8,128)}, f32[6,64,64,128]{3,2,1,0:T(8,128)S(1)}, u32[]{:S(2)}, u32[]{:S(2)}) collective-permute-start(f32[6,64,64,128]{3,2,1,0:T(8,128)} %get-tuple-element.328), channel_id=1, source_target_pairs={{120,0},{0,8},{8,16},{16,24},{24,32},{32,40},{40,48},{48,56},{56,6... | collective-permute-start | bytes 37748744 | tf_op jit(solution)/shard_map/ppermute | solution.py:16
Sparse Core Ops, SparseCore 0:
  989.5 154.0 reduce-scatter.4
where the time goes:
time: 1160 us; the launch traced here: 1150 us
  matrix products  500 us (43%)
  waiting for transfers between devices  428 us (37%)
  other arithmetic  92.2 us (8%)
  loops' own time  68.1 us (6%)
  local copies, waits for them, and re-layouts  49.1 us (4%)
  between operations  13.6 us (1%)
    dot_general x160, matrix products, contract(): return jnp.einsum(form, field, table, precision=lax.Precision.HIGHEST)  500 us
    ppermute x2, waiting for transfers between devices, passed_along(): return lax.ppermute(block, axis, route)  274 us
    unnamed x2, waiting for transfers between devices  154 us
    another operation x1, loops' own time, body(): local_terms, next_terms = lax.fori_loop(0, per_device, step, (empty, empty))  68.1 us
    scatter-add x8, other arithmetic, step(): next_terms = next_terms.at[second].add(cycle_flag * mirrored)  53.8 us
    unnamed x5, local copies, waits for them, and re-layouts  30.8 us
  transfers between devices with their start and end apart: 3, of which 3 were waited for; matrix products, arithmetic and copies ran while one was open for 0% of the time, Pallas kernels for 0%

commit v1 on v0

v1 whole, which is shorter than its diff:
```python
import math

import jax
import jax.numpy as jnp
import ml_dtypes
import numpy as np
from jax import lax
from jax.experimental import pallas as pl
from jax.experimental.pallas import tpu as pltpu
from jax.sharding import PartitionSpec as P

grid_spacing = 0.6
screening = 0.106

f32 = jnp.float32
bf16 = jnp.bfloat16
NX = 64
NY = 64
NZ = 128
ROWS = NX * NY
VMEM_LIMIT = 56 * 2**20
MESH = pl.DeviceIdType.MESH


def signed_freq(count):
    steps = np.arange(count)
    signed = np.where(steps <= count // 2, steps, steps - count)
    return signed * (2.0 * math.pi / (count * grid_spacing))


def screened_kernel():
    fx, fy, fz = signed_freq(NX), signed_freq(NY), signed_freq(NZ)
    square = fy[:, None, None] ** 2 + fx[None, :, None] ** 2 + fz[None, None, :] ** 2
    safe = np.where(square > 0, square, 1.0)
    value = 4.0 * math.pi / safe * -np.expm1(-safe / (4.0 * screening * screening))
    value = np.where(square > 0, value, math.pi / (screening * screening))
    value = (value * (-1.0 / (NX * NY * NZ))).astype(np.float32)
    return jnp.asarray(value.reshape(ROWS, NZ))


def cas(count):
    k = np.arange(count)
    angles = 2.0 * np.pi * ((k[:, None] * k[None, :]) % count) / count
    return np.cos(angles) + np.sin(angles)


def split_table(table):
    high = table.astype(ml_dtypes.bfloat16)
    low = (table - high.astype(np.float64)).astype(ml_dtypes.bfloat16)
    return high, low


def tables():
    high, low = split_table(cas(NZ))
    along_z = np.block([[high, low], [high, low]])
    high, low = split_table(cas(NY))
    zero = np.zeros_like(high)
    high = np.block([[high, zero], [zero, high]])
    low = np.block([[low, zero], [zero, low]])
    along_rows = np.block([[high, high], [low, low]])
    return jnp.asarray(along_z), jnp.asarray(along_rows)


def split(value):
    high = value.astype(bf16)
    low = (value - high.astype(f32)).astype(bf16)
    return high, low


def lanes_stage(value, table):
    high, low = split(value)
    out = jnp.dot(jnp.concatenate([high, low], axis=1), table, preferred_element_type=f32)
    return out[:, :NZ] + out[:, NZ:]


def rows_stage(tile, table):
    high, low = split(tile)
    out = jnp.dot(table, jnp.concatenate([high, low], axis=0), preferred_element_type=f32)
    return out[:128] + out[128:]


def to_tile(value):
    return jnp.concatenate([value[:128], value[128:]], axis=1)


def from_tile(tile):
    return jnp.concatenate([tile[:, :128], tile[:, 128:]], axis=0)


def forward(load, table_z, table_r, first_ref):
    def step(i, _):
        rows = pl.ds(pl.multiple_of(i * 256, 256), 256)
        value = lanes_stage(load(rows), table_z)
        first_ref[rows, :] = from_tile(rows_stage(to_tile(value), table_r))
        return 0

    lax.fori_loop(0, 16, step, 0, unroll=16)


def middle(kernel_ref, table_r, first_ref, second_ref):
    def step(i, _):
        c = [first_ref[pl.ds(i * 4 + q, 64, stride=64), :] for q in range(4)]
        left = jnp.concatenate([c[0], c[1]], axis=0)
        right = jnp.concatenate([c[2], c[3]], axis=0)
        tile = rows_stage(jnp.concatenate([left, right], axis=1), table_r)
        rows = pl.ds(pl.multiple_of(i * 256, 256), 256)
        tile = tile * to_tile(kernel_ref[rows, :])
        value = from_tile(rows_stage(tile, table_r))
        for q in range(4):
            second_ref[pl.ds(i * 4 + q, 64, stride=64), :] = value[q * 64 : (q + 1) * 64]
        return 0

    lax.fori_loop(0, 16, step, 0, unroll=16)


def backward(emit, table_z, table_r, second_ref):
    def step(i, _):
        rows = pl.ds(pl.multiple_of(i * 256, 256), 256)
        tile = rows_stage(to_tile(second_ref[rows, :]), table_r)
        emit(i, rows, lanes_stage(from_tile(tile), table_z))
        return 0

    lax.fori_loop(0, 16, step, 0, unroll=16)


def fused_kernel(
    orb_ref, kernel_in, z_ref, r_ref, out_ref,
    held, sums, first_ref, second_ref, kernel_ref,
    half_up, half_down, full_up, full_down, across,
    load_sem, in_send, in_recv, ring_send, ring_recv, flip_send, flip_recv, out_sem,
):
    band, pair = lax.axis_index("band"), lax.axis_index("pair")
    y, h = pair // 2, pair % 2
    last = y // 3
    odd = band % 2
    twin = band + 1 - 2 * odd
    beyond = (band + 15 + 2 * odd) % 16
    target = beyond + last * (twin - beyond)
    target_h = (1 - h) + last * (2 * h - 1)
    twin_id = (twin, pair)
    near_id = (target, pair)
    far_id = (target, y * 2 + target_h)
    up_id = (band, ((y + 1) % 4) * 2 + h)
    down_id = (band, ((y + 3) % 4) * 2 + h)
    flip_id = (band, y * 2 + 1 - h)

    def load(source, slot):
        return pltpu.make_async_copy(orb_ref.at[source], held.at[slot], load_sem.at[slot])

    loads = [load(3 * h + s, s) for s in range(3)] + [load(3 * (1 - h) + y - last, 3)]
    table_load = pltpu.make_async_copy(kernel_in, kernel_ref, load_sem.at[4])
    for copy in loads[:3]:
        copy.start()
    table_load.start()
    loads[3].start()

    barrier = pltpu.get_barrier_semaphore()
    for other in (twin_id, near_id, far_id, up_id, down_id, flip_id):
        pl.semaphore_signal(barrier, inc=1, device_id=other, device_id_type=MESH)
    pl.semaphore_wait(barrier, 6)

    def remote(source, target_ref, sends, receives, index, device):
        return pltpu.make_async_remote_copy(
            src_ref=source, dst_ref=target_ref, send_sem=sends.at[index], recv_sem=receives.at[index],
            device_id=device, device_id_type=MESH,
        )

    def half_in(source, slot, half, index, device):
        rows = pl.ds(half * 2048, 2048)
        return remote(orb_ref.at[source, rows, :], held.at[slot, rows, :], in_send, in_recv, index, device)

    from_twin = remote(orb_ref.at[y], held.at[4], in_send, in_recv, 0, twin_id)
    one = 2 * y - 2 * last
    first_in = [half_in(one, 5, 0, 1, near_id), half_in(one, 5, 1, 2, far_id)]
    second_in = [half_in(one + 1, 6, 0, 3, near_id), half_in(one + 1, 6, 1, 4, far_id)]
    from_twin.start()
    for copy in first_in:
        copy.start()

    sums[...] = jnp.zeros_like(sums)
    table_z, table_r = z_ref[...], r_ref[...]
    for copy in loads[:3]:
        copy.wait()
    table_load.wait()

    quarter = [pl.multiple_of(((y + q) % 4) * 1024, 1024) for q in range(4)]

    def ring(v, k):
        start, count, target_ref = (
            (quarter[2], 512, half_up),
            (quarter[2] + 512, 512, half_down),
            (quarter[1], 1024, full_up),
            (quarter[3], 1024, full_down),
        )[k]
        rows = pl.ds(pl.multiple_of(start, 512), count)
        device = (up_id, down_id)[k % 2]
        return remote(sums.at[v, rows, :], target_ref.at[v], ring_send, ring_recv, 4 * v + k, device)

    def flip(v):
        rows = pl.ds(pl.multiple_of(quarter[0] + (1 - h) * 512, 512), 512)
        return remote(sums.at[v, rows, :], across.at[v], flip_send, flip_recv, v, flip_id)

    def mine(v):
        rows = pl.ds(pl.multiple_of(quarter[0] + h * 512, 512), 512)
        return pltpu.make_async_copy(sums.at[v, rows, :], out_ref.at[3 * h + v], out_sem.at[v])

    def theirs(v):
        return pltpu.make_async_copy(across.at[v], out_ref.at[3 * (1 - h) + v], out_sem.at[3 + v])

    def ring_start(v):
        ring(v, 0).start()
        ring(v, 1).start()

    def ring_pass(v):
        ring(v, 0).wait_recv()
        rows = pl.ds(quarter[1], 512)
        sums[v, rows, :] += half_up[v]
        ring(v, 2).start()
        ring(v, 1).wait_recv()
        rows = pl.ds(quarter[3] + 512, 512)
        sums[v, rows, :] += half_down[v]
        ring(v, 3).start()

    def ring_end(v):
        ring(v, 2).wait_recv()
        ring(v, 3).wait_recv()
        rows = pl.ds(pl.multiple_of(quarter[0] + (1 - h) * 512, 512), 512)
        part = pl.ds(pl.multiple_of((1 - h) * 512, 512), 512)
        sums[v, rows, :] += full_up[v, part, :] + full_down[v, part, :]
        flip(v).start()
        rows = pl.ds(pl.multiple_of(quarter[0] + h * 512, 512), 512)
        part = pl.ds(pl.multiple_of(h * 512, 512), 512)
        sums[v, rows, :] += full_up[v, part, :] + full_down[v, part, :]
        mine(v).start()

    def solve(a, b, emit):
        forward(lambda rows: held[a, rows, :] * held[b, rows, :], table_z, table_r, first_ref)
        middle(kernel_ref, table_r, first_ref, second_ref)
        backward(emit, table_z, table_r, second_ref)

    @pl.when(y < 3)
    def _():
        a = y // 2
        b = (1 + (y + 1) // 2) * (1 - last)

        def emit(i, rows, value):
            sums[a, rows, :] += held[b, rows, :] * value
            sums[b, rows, :] += held[a, rows, :] * value

        solve(a, b, emit)

    loads[3].wait()

    def edge(e, _):
        late = e // 6
        a = (1 - late) * (e % 3) + late * ((e // 2) % 3)
        twin_part = (e // 3) % 2
        b = (1 - late) * ((1 - twin_part) * (last * a + (1 - last) * 3) + twin_part * 4) + late * (5 + e % 2)

        @pl.when(e == 3)
        def _():
            from_twin.wait_recv()
            for copy in second_in:
                copy.start()

        @pl.when(e == 6)
        def _():
            for copy in first_in:
                copy.wait_recv()

        @pl.when(e == 7)
        def _():
            for copy in second_in:
                copy.wait_recv()

        def emit(i, rows, value):
            sums[a, rows, :] += held[b, rows, :] * value

        solve(a, b, emit)

        @pl.when(e == 7)
        def _():
            ring_start(0)

        @pl.when(e == 8)
        def _():
            ring_pass(0)

        @pl.when(e == 9)
        def _():
            ring_start(1)

        @pl.when(e == 10)
        def _():
            ring_end(0)
            ring_pass(1)

        return 0

    lax.fori_loop(0, 12, edge, 0)
    ring_start(2)
    ring_end(1)
    ring_pass(2)
    ring_end(2)
    for v in range(3):
        flip(v).wait_recv()
        theirs(v).start()
    from_twin.wait_send()
    for copy in first_in + second_in:
        copy.wait_send()
    for v in range(3):
        for k in range(4):
            ring(v, k).wait_send()
        flip(v).wait_send()
        mine(v).wait()
        theirs(v).wait()


def body(orbitals):
    flat = orbitals.reshape(6, ROWS, NZ)
    table_z, table_r = tables()
    anywhere = pl.BlockSpec(memory_space=pl.ANY)
    resident = pl.BlockSpec(memory_space=pltpu.VMEM)

    def buffer(*shape):
        return pltpu.VMEM(shape, f32)

    out = pl.pallas_call(
        fused_kernel,
        out_shape=jax.ShapeDtypeStruct((6, 512, NZ), f32),
        in_specs=[anywhere, anywhere, resident, resident],
        out_specs=anywhere,
        scratch_shapes=[
            buffer(7, ROWS, NZ),
            buffer(3, ROWS, NZ),
            buffer(ROWS, NZ),
            buffer(ROWS, NZ),
            buffer(ROWS, NZ),
            buffer(3, 512, NZ),
            buffer(3, 512, NZ),
            buffer(3, 1024, NZ),
            buffer(3, 1024, NZ),
            buffer(3, 512, NZ),
            pltpu.SemaphoreType.DMA((5,)),
            pltpu.SemaphoreType.DMA((5,)),
            pltpu.SemaphoreType.DMA((5,)),
            pltpu.SemaphoreType.DMA((12,)),
            pltpu.SemaphoreType.DMA((12,)),
            pltpu.SemaphoreType.DMA((3,)),
            pltpu.SemaphoreType.DMA((3,)),
            pltpu.SemaphoreType.DMA((6,)),
        ],
        compiler_params=pltpu.CompilerParams(
            vmem_limit_bytes=VMEM_LIMIT, collective_id=0, has_side_effects=True
        ),
        cost_estimate=pl.CostEstimate(flops=65 * 10**9, bytes_accessed=30 * 10**6, transcendentals=0),
    )(flat, screened_kernel(), table_z, table_r)
    return out.reshape(6, 8, NY, NZ)


def solution(mesh):
    return jax.shard_map(
        body,
        mesh=mesh,
        in_specs=(P("band", None, None, None),),
        out_specs=P("band", "pair", None, None),
        check_vma=False,
    )
```

time: 1160 us -> 130 us (0.11)
  matrix products: 500 us -> 0 us
  waiting for transfers between devices: 428 us -> 0 us
  Pallas kernels: 0 us -> 126 us
  other arithmetic: 92.2 us -> 0 us
  loops' own time: 68.1 us -> 0 us
  local copies, waits for them, and re-layouts: 49.1 us -> 2.73 us
  between operations: 13.6 us -> 0.01 us
    dot_general x160 -> x0, matrix products: 500 us -> none  [contract(): return jnp.einsum(form, field, table, precision=lax.Precision.HIGHEST)]
    ppermute x2 -> x0, waiting for transfers between devices: 274 us -> none  [passed_along(): return lax.ppermute(block, axis, route)]
    unnamed x2 -> x0, waiting for transfers between devices: 154 us -> none
    pallas_call x0 -> x1, Pallas kernels: none -> 126 us  [body(): pl.pallas_call(fused_kernel, out_shape=jax.ShapeDtypeStruct((6, 512, NZ),...]
    another operation x1 -> x0, loops' own time: 68.1 us -> none  [body(): local_terms, next_terms = lax.fori_loop(0, per_device, step, (empty, empty))]
    scatter-add x8 -> x0, other arithmetic: 53.8 us -> none  [step(): next_terms = next_terms.at[second].add(cycle_flag * mirrored)]
    unnamed x5 -> x1, local copies, waits for them, and re-layouts: 30.8 us -> 2.73 us
    select_n x8 -> x0, other arithmetic: 20.9 us -> none  [step(): jnp.where(kind == 1, lax.dynamic_index_in_dim(partner, second, 0, keepdim...]
  transfers between devices with their start and end apart: 3 -> 0, of which waited for: 3 -> 0; matrix products, arithmetic and copies ran while one was open for 0% -> 0% of each run, Pallas kernels for 0% -> 0%
where the time goes in v1:
time: 130 us; the launch traced here: 129 us
  Pallas kernels  126 us (97%)
  local copies, waits for them, and re-layouts  2.73 us (2%)
    pallas_call x1, Pallas kernels, body(): pl.pallas_call(fused_kernel, out_shape=jax.ShapeDtypeStruct((6, 512, NZ),...  126 us
    unnamed x1, local copies, waits for them, and re-layouts  2.73 us

profile of v1, /device:TPU:6, one launch (start us, length us, event | category | flops | bytes accessed | tf_op | source)
XLA Modules:
  0.0 129.2 jit_solution(17591333769746657905)
XLA Ops:
  0.0 126.4 %shard_map.46 = f32[6,512,128]{2,1,0:T(8,128)} custom-call(f32[6,4096,128]{2,1,0:T(8,128)} %bitcast.3, f32[4096,128]{1,0:T(8,128)} %constant.8.clone.kernel_in, bf16[256,256]{1,0:T(8,128)(2,1)} %constant.6.clone.z_ref, bf16[256,256]{1,0:T(8,128)(2,1)} %constant.7.clone.r_ref), custom_call_target="tpu_custom_call" | custom-call | flops 65000001536 | bytes 30000000 | tf_op jit(solution)/shard_map/pallas_call | solution.py:328
  126.4 2.7 %copy.6 = f32[6,8,64,128]{3,2,1,0:T(8,128)} copy(f32[6,8,64,128]{3,2,1,0:T(8,128)} %bitcast.2) | data formatting | bytes 3145728

commit v2 on v1

--- a/solution.py
+++ b/solution.py
@@ -91,7 +91,9 @@
     def step(i, _):
         rows = pl.ds(pl.multiple_of(i * 256, 256), 256)
         value = lanes_stage(load(rows), table_z)
-        first_ref[rows, :] = from_tile(rows_stage(to_tile(value), table_r))
+        value = from_tile(rows_stage(to_tile(value), table_r))
+        for q in range(4):
+            first_ref[pl.ds(i * 4 + q, 64, stride=64), :] = value[q * 64 : (q + 1) * 64]
         return 0
 
     lax.fori_loop(0, 16, step, 0, unroll=16)
@@ -99,11 +101,8 @@
 
 def middle(kernel_ref, table_r, first_ref, second_ref):
     def step(i, _):
-        c = [first_ref[pl.ds(i * 4 + q, 64, stride=64), :] for q in range(4)]
-        left = jnp.concatenate([c[0], c[1]], axis=0)
-        right = jnp.concatenate([c[2], c[3]], axis=0)
-        tile = rows_stage(jnp.concatenate([left, right], axis=1), table_r)
         rows = pl.ds(pl.multiple_of(i * 256, 256), 256)
+        tile = rows_stage(to_tile(first_ref[rows, :]), table_r)
         tile = tile * to_tile(kernel_ref[rows, :])
         value = from_tile(rows_stage(tile, table_r))
         for q in range(4):
@@ -135,11 +134,14 @@
     odd = band % 2
     twin = band + 1 - 2 * odd
     beyond = (band + 15 + 2 * odd) % 16
-    target = beyond + last * (twin - beyond)
-    target_h = (1 - h) + last * (2 * h - 1)
+    crossing = (y + odd) % 2
+    target = twin + crossing * (beyond - twin)
+    target_h = h + crossing * (1 - 2 * h)
     twin_id = (twin, pair)
-    near_id = (target, pair)
-    far_id = (target, y * 2 + target_h)
+    near_id = (beyond, pair)
+    far_id = (beyond, y * 2 + 1 - h)
+    near_two_id = (target, pair)
+    far_two_id = (target, y * 2 + target_h)
     up_id = (band, ((y + 1) % 4) * 2 + h)
     down_id = (band, ((y + 3) % 4) * 2 + h)
     flip_id = (band, y * 2 + 1 - h)
@@ -170,9 +172,8 @@
         return remote(orb_ref.at[source, rows, :], held.at[slot, rows, :], in_send, in_recv, index, device)
 
     from_twin = remote(orb_ref.at[y], held.at[4], in_send, in_recv, 0, twin_id)
-    one = 2 * y - 2 * last
-    first_in = [half_in(one, 5, 0, 1, near_id), half_in(one, 5, 1, 2, far_id)]
-    second_in = [half_in(one + 1, 6, 0, 3, near_id), half_in(one + 1, 6, 1, 4, far_id)]
+    first_in = [half_in(y, 5, 0, 1, near_id), half_in(y, 5, 1, 2, far_id)]
+    second_in = [half_in(4 + y // 2, 6, 0, 3, near_two_id), half_in(4 + y // 2, 6, 1, 4, far_two_id)]
     from_twin.start()
     for copy in first_in:
         copy.start()
@@ -252,23 +253,26 @@
     loads[3].wait()
 
     def edge(e, _):
-        late = e // 6
-        a = (1 - late) * (e % 3) + late * ((e // 2) % 3)
-        twin_part = (e // 3) % 2
-        b = (1 - late) * ((1 - twin_part) * (last * a + (1 - last) * 3) + twin_part * 4) + late * (5 + e % 2)
-
-        @pl.when(e == 3)
+        late, odd_step = e // 6, e % 2
+        a = late * ((e + 3) // 3 - 2) + (1 - late) * (1 - odd_step) * (e // 2)
+        own = last * a + (1 - last) * 3
+        b = late * (4 + e % 3) + (1 - late) * (odd_step * (4 + e // 2) + (1 - odd_step) * own)
+
+        @pl.when(e == 1)
         def _():
             from_twin.wait_recv()
+
+        @pl.when(e == 2)
+        def _():
             for copy in second_in:
                 copy.start()
 
-        @pl.when(e == 6)
+        @pl.when(e == 3)
         def _():
             for copy in first_in:
                 copy.wait_recv()
 
-        @pl.when(e == 7)
+        @pl.when(e == 5)
         def _():
             for copy in second_in:
                 copy.wait_recv()
@@ -278,21 +282,21 @@
 
         solve(a, b, emit)
 
-        @pl.when(e == 7)
+        @pl.when(e == 5)
         def _():
             ring_start(0)
 
+        @pl.when(e == 6)
+        def _():
+            ring_pass(0)
+
         @pl.when(e == 8)
         def _():
-            ring_pass(0)
+            ring_start(1)
+            ring_end(0)
 
         @pl.when(e == 9)
         def _():
-            ring_start(1)
-
-        @pl.when(e == 10)
-        def _():
-            ring_end(0)
             ring_pass(1)
 
         return 0

time: 130 us -> 125 us (0.962)
  Pallas kernels: 126 us -> 123 us
    pallas_call x1, Pallas kernels: 126 us -> 123 us  [body(): pl.pallas_call(fused_kernel, out_shape=jax.ShapeDtypeStruct((6, 512, NZ),...]
where the time goes in v2:
time: 125 us
  Pallas kernels  123 us (98%)
  local copies, waits for them, and re-layouts  2.73 us (2%)
    pallas_call x1, Pallas kernels, body(): pl.pallas_call(fused_kernel, out_shape=jax.ShapeDtypeStruct((6, 512, NZ),...  123 us
    unnamed x1, local copies, waits for them, and re-layouts  2.73 us

profile of v2, /device:TPU:6, one launch (start us, length us, event | category | flops | bytes accessed | tf_op | source)
XLA Modules:
  0.0 125.3 jit_solution(4992086387686319368)
XLA Ops:
  0.0 122.6 %shard_map.46 = f32[6,512,128]{2,1,0:T(8,128)} custom-call(f32[6,4096,128]{2,1,0:T(8,128)} %bitcast.3, f32[4096,128]{1,0:T(8,128)} %constant.8.clone.kernel_in, bf16[256,256]{1,0:T(8,128)(2,1)} %constant.6.clone.z_ref, bf16[256,256]{1,0:T(8,128)(2,1)} %constant.7.clone.r_ref), custom_call_target="tpu_custom_call" | custom-call | flops 65000001536 | bytes 30000000 | tf_op jit(solution)/shard_map/pallas_call | solution.py:332
  122.6 2.7 %copy.6 = f32[6,8,64,128]{3,2,1,0:T(8,128)} copy(f32[6,8,64,128]{3,2,1,0:T(8,128)} %bitcast.2) | data formatting | bytes 3145728

commit v3 on v2

--- a/solution.py
+++ b/solution.py
@@ -235,9 +235,22 @@
         mine(v).start()
 
     def solve(a, b, emit):
-        forward(lambda rows: held[a, rows, :] * held[b, rows, :], table_z, table_r, first_ref)
-        middle(kernel_ref, table_r, first_ref, second_ref)
-        backward(emit, table_z, table_r, second_ref)
+        def phase(k, _):
+            @pl.when(k == 0)
+            def _():
+                forward(lambda rows: held[a, rows, :] * held[b, rows, :], table_z, table_r, first_ref)
+
+            @pl.when(k == 1)
+            def _():
+                middle(kernel_ref, table_r, first_ref, second_ref)
+
+            @pl.when(k == 2)
+            def _():
+                backward(emit, table_z, table_r, second_ref)
+
+            return 0
+
+        lax.fori_loop(0, 3, phase, 0)
 
     @pl.when(y < 3)
     def _():

time: 125 us -> 126 us (level)
  no operation moved by 1% of the time
where the time goes in v3:
time: 126 us
  Pallas kernels  123 us (98%)
  local copies, waits for them, and re-layouts  2.73 us (2%)
    pallas_call x1, Pallas kernels, body(): pl.pallas_call(fused_kernel, out_shape=jax.ShapeDtypeStruct((6, 512, NZ),...  123 us
    unnamed x1, local copies, waits for them, and re-layouts  2.73 us

profile of v3, /device:TPU:6, one launch (start us, length us, event | category | flops | bytes accessed | tf_op | source)
XLA Modules:
  0.0 125.8 jit_solution(16292260299720564917)
XLA Ops:
  0.0 123.1 %shard_map.46 = f32[6,512,128]{2,1,0:T(8,128)} custom-call(f32[6,4096,128]{2,1,0:T(8,128)} %bitcast.3, f32[4096,128]{1,0:T(8,128)} %constant.8.clone.kernel_in, bf16[256,256]{1,0:T(8,128)(2,1)} %constant.6.clone.z_ref, bf16[256,256]{1,0:T(8,128)(2,1)} %constant.7.clone.r_ref), custom_call_target="tpu_custom_call" | custom-call | flops 65000001536 | bytes 30000000 | tf_op jit(solution)/shard_map/pallas_call | solution.py:345
  123.1 2.7 %copy.6 = f32[6,8,64,128]{3,2,1,0:T(8,128)} copy(f32[6,8,64,128]{3,2,1,0:T(8,128)} %bitcast.2) | data formatting | bytes 3145728

commit v4 on v2

--- a/solution.py
+++ b/solution.py
@@ -87,29 +87,37 @@
     return jnp.concatenate([tile[:, :128], tile[:, 128:]], axis=0)
 
 
+def store_turned(ref, group, value):
+    turned = jnp.transpose(value.reshape(8, 8, 8, NZ), (1, 2, 0, 3))
+    for high in range(8):
+        for low in range(8):
+            start = (high * 8 + low) * 64 + group * 8
+            ref[pl.ds(pl.multiple_of(start, 8), 8), :] = turned[high, low]
+
+
 def forward(load, table_z, table_r, first_ref):
     def step(i, _):
-        rows = pl.ds(pl.multiple_of(i * 256, 256), 256)
+        rows = pl.ds(pl.multiple_of(i * 512, 512), 512)
         value = lanes_stage(load(rows), table_z)
-        value = from_tile(rows_stage(to_tile(value), table_r))
-        for q in range(4):
-            first_ref[pl.ds(i * 4 + q, 64, stride=64), :] = value[q * 64 : (q + 1) * 64]
+        halves = [rows_stage(to_tile(value[:256]), table_r), rows_stage(to_tile(value[256:]), table_r)]
+        store_turned(first_ref, i, jnp.concatenate([from_tile(tile) for tile in halves], axis=0))
         return 0
 
-    lax.fori_loop(0, 16, step, 0, unroll=16)
+    lax.fori_loop(0, 8, step, 0, unroll=8)
 
 
 def middle(kernel_ref, table_r, first_ref, second_ref):
     def step(i, _):
-        rows = pl.ds(pl.multiple_of(i * 256, 256), 256)
-        tile = rows_stage(to_tile(first_ref[rows, :]), table_r)
-        tile = tile * to_tile(kernel_ref[rows, :])
-        value = from_tile(rows_stage(tile, table_r))
-        for q in range(4):
-            second_ref[pl.ds(i * 4 + q, 64, stride=64), :] = value[q * 64 : (q + 1) * 64]
+        halves = []
+        for half in range(2):
+            rows = pl.ds(pl.multiple_of(i * 512 + half * 256, 256), 256)
+            tile = rows_stage(to_tile(first_ref[rows, :]), table_r)
+            tile = tile * to_tile(kernel_ref[rows, :])
+            halves.append(from_tile(rows_stage(tile, table_r)))
+        store_turned(second_ref, i, jnp.concatenate(halves, axis=0))
         return 0
 
-    lax.fori_loop(0, 16, step, 0, unroll=16)
+    lax.fori_loop(0, 8, step, 0, unroll=8)
 
 
 def backward(emit, table_z, table_r, second_ref):
@@ -135,13 +143,12 @@
     twin = band + 1 - 2 * odd
     beyond = (band + 15 + 2 * odd) % 16
     crossing = (y + odd) % 2
-    target = twin + crossing * (beyond - twin)
-    target_h = h + crossing * (1 - 2 * h)
     twin_id = (twin, pair)
     near_id = (beyond, pair)
     far_id = (beyond, y * 2 + 1 - h)
-    near_two_id = (target, pair)
-    far_two_id = (target, y * 2 + target_h)
+    aside_y = (y + 3) % 4
+    aside_id = (beyond, aside_y * 2 + 1 - h)
+    aside_from_id = (beyond, ((y + 1) % 4) * 2 + 1 - h)
     up_id = (band, ((y + 1) % 4) * 2 + h)
     down_id = (band, ((y + 3) % 4) * 2 + h)
     flip_id = (band, y * 2 + 1 - h)
@@ -157,23 +164,52 @@
     loads[3].start()
 
     barrier = pltpu.get_barrier_semaphore()
-    for other in (twin_id, near_id, far_id, up_id, down_id, flip_id):
+    for other in (twin_id, near_id, far_id, aside_id, aside_from_id, up_id, down_id, flip_id):
         pl.semaphore_signal(barrier, inc=1, device_id=other, device_id_type=MESH)
-    pl.semaphore_wait(barrier, 6)
-
-    def remote(source, target_ref, sends, receives, index, device):
+    pl.semaphore_wait(barrier, 8)
+
+    def remote(source, target_ref, sends, receives, index, device, arrival=None):
         return pltpu.make_async_remote_copy(
-            src_ref=source, dst_ref=target_ref, send_sem=sends.at[index], recv_sem=receives.at[index],
+            src_ref=source, dst_ref=target_ref, send_sem=sends.at[index],
+            recv_sem=receives.at[index if arrival is None else arrival],
             device_id=device, device_id_type=MESH,
         )
 
-    def half_in(source, slot, half, index, device):
+    def half_in(source, slot, half, index, device, arrival=None):
         rows = pl.ds(half * 2048, 2048)
-        return remote(orb_ref.at[source, rows, :], held.at[slot, rows, :], in_send, in_recv, index, device)
+        return remote(
+            orb_ref.at[source, rows, :], held.at[slot, rows, :], in_send, in_recv, index, device, arrival
+        )
 
     from_twin = remote(orb_ref.at[y], held.at[4], in_send, in_recv, 0, twin_id)
     first_in = [half_in(y, 5, 0, 1, near_id), half_in(y, 5, 1, 2, far_id)]
-    second_in = [half_in(4 + y // 2, 6, 0, 3, near_two_id), half_in(4 + y // 2, 6, 1, 4, far_two_id)]
+    second = 4 + y // 2
+    crossing_in = half_in(second, 6, 0, 3, near_id)
+    staying_in = [half_in(second, 6, 0, 3, twin_id), half_in(second, 6, 1, 4, twin_id)]
+    aside_in = half_in(4 + aside_y // 2, 6, 1, 5, aside_id, 4)
+
+    def second_start():
+        @pl.when(crossing == 1)
+        def _():
+            crossing_in.start()
+
+        @pl.when(crossing == 0)
+        def _():
+            aside_in.start()
+            for copy in staying_in:
+                copy.start()
+
+    def second_sent():
+        @pl.when(crossing == 1)
+        def _():
+            crossing_in.wait_send()
+
+        @pl.when(crossing == 0)
+        def _():
+            aside_in.wait_send()
+            for copy in staying_in:
+                copy.wait_send()
+
     from_twin.start()
     for copy in first_in:
         copy.start()
@@ -264,8 +300,7 @@
 
         @pl.when(e == 2)
         def _():
-            for copy in second_in:
-                copy.start()
+            second_start()
 
         @pl.when(e == 3)
         def _():
@@ -274,7 +309,7 @@
 
         @pl.when(e == 5)
         def _():
-            for copy in second_in:
+            for copy in staying_in:
                 copy.wait_recv()
 
         def emit(i, rows, value):
@@ -310,8 +345,9 @@
         flip(v).wait_recv()
         theirs(v).start()
     from_twin.wait_send()
-    for copy in first_in + second_in:
+    for copy in first_in:
         copy.wait_send()
+    second_sent()
     for v in range(3):
         for k in range(4):
             ring(v, k).wait_send()
@@ -346,7 +382,7 @@
             buffer(3, 1024, NZ),
             buffer(3, 512, NZ),
             pltpu.SemaphoreType.DMA((5,)),
-            pltpu.SemaphoreType.DMA((5,)),
+            pltpu.SemaphoreType.DMA((6,)),
             pltpu.SemaphoreType.DMA((5,)),
             pltpu.SemaphoreType.DMA((12,)),
             pltpu.SemaphoreType.DMA((12,)),

time: 125 us -> 126 us (level); the launches traced: 125 us -> 125 us
  no operation moved by 1% of the time
where the time goes in v4:
time: 126 us; the launch traced here: 125 us
  Pallas kernels  122 us (97%)
  local copies, waits for them, and re-layouts  2.73 us (2%)
    pallas_call x1, Pallas kernels, body(): pl.pallas_call(fused_kernel, out_shape=jax.ShapeDtypeStruct((6, 512, NZ),...  122 us
    unnamed x1, local copies, waits for them, and re-layouts  2.73 us

profile of v4, /device:TPU:6, one launch (start us, length us, event | category | flops | bytes accessed | tf_op | source)
XLA Modules:
  0.0 124.6 jit_solution(18124123017843838867)
XLA Ops:
  0.0 121.8 %shard_map.46 = f32[6,512,128]{2,1,0:T(8,128)} custom-call(f32[6,4096,128]{2,1,0:T(8,128)} %bitcast.3, f32[4096,128]{1,0:T(8,128)} %constant.8.clone.kernel_in, bf16[256,256]{1,0:T(8,128)(2,1)} %constant.6.clone.z_ref, bf16[256,256]{1,0:T(8,128)(2,1)} %constant.7.clone.r_ref), custom_call_target="tpu_custom_call" | custom-call | flops 65000001536 | bytes 30000000 | tf_op jit(solution)/shard_map/pallas_call | solution.py:368
  121.8 2.7 %copy.6 = f32[6,8,64,128]{3,2,1,0:T(8,128)} copy(f32[6,8,64,128]{3,2,1,0:T(8,128)} %bitcast.2) | data formatting | bytes 3145728

commit v5 on v4

v5 whole, which is shorter than its diff:
```python
import math

import jax
import jax.numpy as jnp
import ml_dtypes
import numpy as np
from jax import lax
from jax.experimental import pallas as pl
from jax.experimental.pallas import tpu as pltpu
from jax.sharding import PartitionSpec as P

grid_spacing = 0.6
screening = 0.106

f32 = jnp.float32
bf16 = jnp.bfloat16
NX = 64
NY = 64
NZ = 128
ROWS = NX * NY
VMEM_LIMIT = 56 * 2**20
MESH = pl.DeviceIdType.MESH


def signed_freq(count):
    steps = np.arange(count)
    signed = np.where(steps <= count // 2, steps, steps - count)
    return signed * (2.0 * math.pi / (count * grid_spacing))


def screened_kernel():
    fx, fy, fz = signed_freq(NX), signed_freq(NY), signed_freq(NZ)
    square = fy[:, None, None] ** 2 + fx[None, :, None] ** 2 + fz[None, None, :] ** 2
    safe = np.where(square > 0, square, 1.0)
    value = 4.0 * math.pi / safe * -np.expm1(-safe / (4.0 * screening * screening))
    value = np.where(square > 0, value, math.pi / (screening * screening))
    value = (value * (-1.0 / (NX * NY * NZ))).astype(np.float32)
    return jnp.asarray(value.reshape(ROWS, NZ))


def cas(count):
    k = np.arange(count)
    angles = 2.0 * np.pi * ((k[:, None] * k[None, :]) % count) / count
    return np.cos(angles) + np.sin(angles)


def split_table(table):
    high = table.astype(ml_dtypes.bfloat16)
    low = (table - high.astype(np.float64)).astype(ml_dtypes.bfloat16)
    return high, low


def tables():
    high, low = split_table(cas(NZ))
    along_z = np.block([[high, low], [high, low]])
    high, low = split_table(cas(NY))
    zero = np.zeros_like(high)
    high = np.block([[high, zero], [zero, high]])
    low = np.block([[low, zero], [zero, low]])
    along_rows = np.block([[high, high], [low, low]])
    return jnp.asarray(along_z), jnp.asarray(along_rows)


def split(value):
    high = value.astype(bf16)
    low = (value - high.astype(f32)).astype(bf16)
    return high, low


def lanes_stage(value, table):
    high, low = split(value)
    out = jnp.dot(jnp.concatenate([high, low], axis=1), table, preferred_element_type=f32)
    return out[:, :NZ] + out[:, NZ:]


def rows_stage(tile, table):
    high, low = split(tile)
    out = jnp.dot(table, jnp.concatenate([high, low], axis=0), preferred_element_type=f32)
    return out[:128] + out[128:]


def to_tile(value):
    return jnp.concatenate([value[:128], value[128:]], axis=1)


def from_tile(tile):
    return jnp.concatenate([tile[:, :128], tile[:, 128:]], axis=0)


def store_turned(ref, group, value):
    turned = jnp.transpose(value.reshape(8, 8, 8, NZ), (1, 2, 0, 3))
    for high in range(8):
        for low in range(8):
            start = (high * 8 + low) * 64 + group * 8
            ref[pl.ds(pl.multiple_of(start, 8), 8), :] = turned[high, low]


def forward(load, table_z, table_r, first_ref):
    def step(i, _):
        rows = pl.ds(pl.multiple_of(i * 512, 512), 512)
        value = lanes_stage(load(rows), table_z)
        halves = [rows_stage(to_tile(value[:256]), table_r), rows_stage(to_tile(value[256:]), table_r)]
        store_turned(first_ref, i, jnp.concatenate([from_tile(tile) for tile in halves], axis=0))
        return 0

    lax.fori_loop(0, 8, step, 0, unroll=8)


def middle(kernel_ref, table_r, first_ref, second_ref):
    def step(i, _):
        halves = []
        for half in range(2):
            rows = pl.ds(pl.multiple_of(i * 512 + half * 256, 256), 256)
            tile = rows_stage(to_tile(first_ref[rows, :]), table_r)
            tile = tile * to_tile(kernel_ref[rows, :])
            halves.append(from_tile(rows_stage(tile, table_r)))
        store_turned(second_ref, i, jnp.concatenate(halves, axis=0))
        return 0

    lax.fori_loop(0, 8, step, 0, unroll=8)


def backward(emit, table_z, table_r, second_ref):
    def step(i, _):
        rows = pl.ds(pl.multiple_of(i * 256, 256), 256)
        tile = rows_stage(to_tile(second_ref[rows, :]), table_r)
        emit(i, rows, lanes_stage(from_tile(tile), table_z))
        return 0

    lax.fori_loop(0, 16, step, 0, unroll=16)


def fused_kernel(
    orb_ref, kernel_in, z_ref, r_ref, out_ref,
    held, sums, first_ref, second_ref, kernel_ref, twin_part, side_part,
    load_sem, owned_send, owned_recv, in_send, in_recv, twin_send, twin_recv, side_send, side_recv,
    out_send, out_recv, out_sem,
):
    band, pair = lax.axis_index("band"), lax.axis_index("pair")
    y, h = pair // 2, pair % 2
    core = band % 2
    side, u = y // 2, y % 2
    home = core * side + (1 - core) * (1 - side)
    twin = band + 1 - 2 * core
    block = band - core + side
    keep = home * h + (1 - home) * (1 - h)
    near_y = y + 1 - 2 * u
    far_y = 3 - y
    twin_id = (twin, pair)
    side_id = (band, near_y * 2 + h)
    across_id = (band, far_y * 2 + h)
    flip_id = (twin, y * 2 + 1 - h)
    corner_id = (twin, far_y * 2 + 1 - h)

    matched = core * (1 - side) + (1 - core) * side
    to_y = matched * y + (1 - matched) * far_y
    to_h = matched * h + (1 - matched) * (1 - h)
    forward_way = 2 * core - 1
    to_home = ((band + 16 + forward_way) % 16, to_y * 2 + to_h)
    to_guest = ((band + 16 + 2 * forward_way) % 16, to_y * 2 + to_h)
    foreign = (band - core + 15 + 3 * side) % 16
    from_same = (foreign, pair)
    from_other = (foreign, far_y * 2 + 1 - h)

    def load(source, slot):
        return pltpu.make_async_copy(orb_ref.at[source], held.at[slot], load_sem.at[slot])

    owned_loads = [load(3 * h + v, v) for v in range(3)]
    loads = [
        load(home * (3 * (1 - h) + 2 * u) + (1 - home) * 3 * u, 3),
        load(home * (3 * (1 - h) + 1) + (1 - home) * (3 * u + 1), 4),
    ]
    guest_load = load(3 * u + 2, 5)
    table_load = pltpu.make_async_copy(kernel_in, kernel_ref, load_sem.at[6])

    @pl.when(home == 1)
    def _():
        for copy in owned_loads:
            copy.start()

    table_load.start()
    for copy in loads:
        copy.start()

    @pl.when(home == 0)
    def _():
        guest_load.start()

    barrier = pltpu.get_barrier_semaphore()
    partners = (twin_id, side_id, across_id, flip_id, corner_id, to_home, to_guest, from_same, from_other)
    for other in partners:
        pl.semaphore_signal(barrier, inc=1, device_id=other, device_id_type=MESH)
    pl.semaphore_wait(barrier, len(partners))

    def remote(source, target_ref, send_sem, recv_sem, device):
        return pltpu.make_async_remote_copy(
            src_ref=source, dst_ref=target_ref, send_sem=send_sem, recv_sem=recv_sem,
            device_id=device, device_id_type=MESH,
        )

    def owned_in(v):
        return remote(orb_ref.at[3 * h + v], held.at[v], owned_send.at[v], owned_recv.at[v], twin_id)

    def foreign_in(j):
        slot = (5, 6, 6)[j]
        rows = pl.ds(pl.multiple_of((1 - matched) * 2048, 2048), 2048)
        source = orb_ref.at[3 * (to_y % 2) + j, rows, :]
        arrival = in_recv.at[(slot - 5) * 2 + 1 - matched]
        return remote(source, held.at[slot, rows, :], in_send.at[j], arrival, to_guest if j == 2 else to_home)

    def foreign_wait(slot):
        for half in range(2):
            rows = pl.ds(half * 2048, 2048)
            ref = held.at[slot, rows, :]
            remote(ref, ref, in_send.at[0], in_recv.at[(slot - 5) * 2 + half], from_same).wait_recv()

    @pl.when(home == 1)
    def _():
        for v in range(3):
            owned_in(v).start()

    for j in (0, 2, 1):
        foreign_in(j).start()

    for v in range(3):
        sums[v] = jnp.zeros(sums.shape[1:], f32)
    table_z, table_r = z_ref[...], r_ref[...]

    @pl.when(home == 1)
    def _():
        for copy in owned_loads:
            copy.wait()

    @pl.when(home == 0)
    def _():
        owned_in(0).wait_recv()

    table_load.wait()

    def twin_copy(v):
        return remote(sums.at[v, :, 1 - keep], twin_part.at[v], twin_send.at[v], twin_recv.at[v], twin_id)

    def side_copy(v, k):
        row = (near_y, 3 - near_y)[k]
        index = 2 * v + k
        return remote(sums.at[v, row, keep], side_part.at[v, k], side_send.at[index], side_recv.at[index], side_id)

    def out_copy(v, k):
        row = (y, far_y)[k]
        return remote(
            sums.at[v, row, keep], out_ref.at[3 * h + v], out_send.at[2 * v + k], out_recv.at[3 * h + v],
            (block, row * 2 + keep),
        )

    def out_local(v):
        return pltpu.make_async_copy(sums.at[v, y, keep], out_ref.at[3 * h + v], out_sem.at[v])

    def pass_on(v):
        twin_copy(v).wait_recv()
        for k, row in enumerate((near_y, 3 - near_y)):
            sums[v, row, keep] += twin_part[v, row]
            side_copy(v, k).start()

    def finish(v):
        for k, row in ((1, far_y), (0, y)):
            side_copy(v, k).wait_recv()
            sums[v, row, keep] += twin_part[v, row] + side_part[v, k]
            if k == 1:
                out_copy(v, 1).start()
            else:

                @pl.when(home == 1)
                def _():
                    out_local(v).start()

                @pl.when(home == 0)
                def _():
                    out_copy(v, 0).start()

    def place(i):
        return i // 4, (i // 2) % 2, pl.ds(pl.multiple_of((i % 2) * 256, 256), 256)

    def solve(a, b, emit):
        forward(lambda rows: held[a, rows, :] * held[b, rows, :], table_z, table_r, first_ref)
        middle(kernel_ref, table_r, first_ref, second_ref)
        backward(emit, table_z, table_r, second_ref)

    def both(a, _):
        b = 2 - u

        def emit(i, rows, value):
            q, half, part = place(i)
            sums[a, q, half, part, :] += held[b, rows, :] * value
            sums[b, q, half, part, :] += held[a, rows, :] * value

        solve(a, b, emit)
        return 0

    lax.fori_loop(0, home * (2 - u), both, 0)
    for copy in loads:
        copy.wait()

    def edge(e, _):
        late = e // 8
        a = late * 2 + (1 - late) * ((e // 2) % 2)
        slot = late * (3 + e % 4) + (1 - late) * (3 + 2 * (e // 4) + e % 2)
        itself = home * u * ((7 - slot) // 3 - (6 - slot) // 3)
        b = slot + itself * (a - slot)

        @pl.when(e == 4)
        def _():
            @pl.when(home == 1)
            def _():
                foreign_wait(5)

            @pl.when(home == 0)
            def _():
                guest_load.wait()

        @pl.when(e == 5)
        def _():
            foreign_wait(6)

        @pl.when((1 - home) * e == 2)
        def _():
            owned_in(1).wait_recv()

        @pl.when((1 - home) * e == 8)
        def _():
            owned_in(2).wait_recv()

        def emit(i, rows, value):
            q, half, part = place(i)
            sums[a, q, half, part, :] += held[b, rows, :] * value

        solve(a, b, emit)

        @pl.when(e == 5)
        def _():
            twin_copy(0).start()

        @pl.when(e == 6)
        def _():
            pass_on(0)

        @pl.when(e == 7)
        def _():
            twin_copy(1).start()

        @pl.when(e == 8)
        def _():
            pass_on(1)

        @pl.when(e == 9)
        def _():
            finish(0)

        @pl.when(e == 11)
        def _():
            twin_copy(2).start()

        return 0

    lax.fori_loop(0, 12, edge, 0)
    pass_on(2)
    finish(1)
    finish(2)

    for v in range(3):
        remote(sums.at[v, y, keep], out_ref.at[3 * (1 - h) + v], out_send.at[0], out_recv.at[3 * (1 - h) + v], flip_id).wait_recv()

    @pl.when(home == 0)
    def _():
        for v in range(3):
            remote(sums.at[v, y, keep], out_ref.at[3 * h + v], out_send.at[0], out_recv.at[3 * h + v], flip_id).wait_recv()
            out_copy(v, 0).wait_send()

    @pl.when(home == 1)
    def _():
        for v in range(3):
            owned_in(v).wait_send()
            out_local(v).wait()

    for v in range(3):
        foreign_in(v).wait_send()
        twin_copy(v).wait_send()
        side_copy(v, 0).wait_send()
        side_copy(v, 1).wait_send()
        out_copy(v, 1).wait_send()


def body(orbitals):
    flat = orbitals.reshape(6, ROWS, NZ)
    table_z, table_r = tables()
    anywhere = pl.BlockSpec(memory_space=pl.ANY)
    resident = pl.BlockSpec(memory_space=pltpu.VMEM)

    def buffer(*shape):
        return pltpu.VMEM(shape, f32)

    out = pl.pallas_call(
        fused_kernel,
        out_shape=jax.ShapeDtypeStruct((6, 512, NZ), f32),
        in_specs=[anywhere, anywhere, resident, resident],
        out_specs=anywhere,
        scratch_shapes=[
            buffer(7, ROWS, NZ),
            buffer(3, 4, 2, 512, NZ),
            buffer(ROWS, NZ),
            buffer(ROWS, NZ),
            buffer(ROWS, NZ),
            buffer(3, 4, 512, NZ),
            buffer(3, 2, 512, NZ),
        ]
        + [pltpu.SemaphoreType.DMA((count,)) for count in (7, 3, 3, 3, 4, 3, 3, 6, 6, 6, 6, 3)],
        compiler_params=pltpu.CompilerParams(
            vmem_limit_bytes=VMEM_LIMIT, collective_id=0, has_side_effects=True
        ),
        cost_estimate=pl.CostEstimate(flops=65 * 10**9, bytes_accessed=30 * 10**6, transcendentals=0),
    )(flat, screened_kernel(), table_z, table_r)
    return out.reshape(6, 8, NY, NZ)


def solution(mesh):
    return jax.shard_map(
        body,
        mesh=mesh,
        in_specs=(P("band", None, None, None),),
        out_specs=P("band", "pair", None, None),
        check_vma=False,
    )
```

time: 126 us -> 103 us (0.82)
  Pallas kernels: 122 us -> 98.6 us
    pallas_call x1, Pallas kernels: 122 us -> 98.6 us  [body(): pl.pallas_call(fused_kernel, out_shape=jax.ShapeDtypeStruct((6, 512, NZ),...]
where the time goes in v5:
time: 103 us; the launch traced here: 101 us
  Pallas kernels  98.6 us (96%)
  local copies, waits for them, and re-layouts  2.73 us (3%)
    pallas_call x1, Pallas kernels, body(): pl.pallas_call(fused_kernel, out_shape=jax.ShapeDtypeStruct((6, 512, NZ),...  98.6 us
    unnamed x1, local copies, waits for them, and re-layouts  2.73 us

profile of v5, /device:TPU:6, one launch (start us, length us, event | category | flops | bytes accessed | tf_op | source)
XLA Modules:
  0.0 101.3 jit_solution(5075253171987424484)
XLA Ops:
  0.0 98.6 %shard_map.46 = f32[6,512,128]{2,1,0:T(8,128)} custom-call(f32[6,4096,128]{2,1,0:T(8,128)} %bitcast.3, f32[4096,128]{1,0:T(8,128)} %constant.8.clone.kernel_in, bf16[256,256]{1,0:T(8,128)(2,1)} %constant.6.clone.z_ref, bf16[256,256]{1,0:T(8,128)(2,1)} %constant.7.clone.r_ref), custom_call_target="tpu_custom_call" | custom-call | flops 65000001536 | bytes 30000000 | tf_op jit(solution)/shard_map/pallas_call | solution.py:401
  98.6 2.7 %copy.6 = f32[6,8,64,128]{3,2,1,0:T(8,128)} copy(f32[6,8,64,128]{3,2,1,0:T(8,128)} %bitcast.2) | data formatting | bytes 3145728

commit v6 on v5

--- a/solution.py
+++ b/solution.py
@@ -219,7 +219,7 @@
         for v in range(3):
             owned_in(v).start()
 
-    for j in (0, 2, 1):
+    for j in (0, 2):
         foreign_in(j).start()
 
     for v in range(3):
@@ -257,7 +257,7 @@
 
     def pass_on(v):
         twin_copy(v).wait_recv()
-        for k, row in enumerate((near_y, 3 - near_y)):
+        for k, row in ((1, 3 - near_y), (0, near_y)):
             sums[v, row, keep] += twin_part[v, row]
             side_copy(v, k).start()
 
@@ -285,27 +285,31 @@
         middle(kernel_ref, table_r, first_ref, second_ref)
         backward(emit, table_z, table_r, second_ref)
 
-    def both(a, _):
-        b = 2 - u
-
+    def both(a, b):
         def emit(i, rows, value):
             q, half, part = place(i)
             sums[a, q, half, part, :] += held[b, rows, :] * value
             sums[b, q, half, part, :] += held[a, rows, :] * value
 
         solve(a, b, emit)
-        return 0
-
-    lax.fori_loop(0, home * (2 - u), both, 0)
+
     for copy in loads:
         copy.wait()
 
     def edge(e, _):
-        late = e // 8
-        a = late * 2 + (1 - late) * ((e // 2) % 2)
-        slot = late * (3 + e % 4) + (1 - late) * (3 + 2 * (e // 4) + e % 2)
+        late, mid = e // 8, (e // 4) % 2
+        a = late * 2 + (1 - late) * ((1 - mid) * ((e // 2) % 2) + mid * (e % 2))
+        slot = 3 + late * (e % 4) + (1 - late) * ((1 - mid) * (e % 2) + mid * (2 + (e // 2) % 2))
         itself = home * u * ((7 - slot) // 3 - (6 - slot) // 3)
         b = slot + itself * (a - slot)
+
+        @pl.when((1 - home) * e == 2)
+        def _():
+            owned_in(1).wait_recv()
+
+        @pl.when(e == 3)
+        def _():
+            foreign_in(1).start()
 
         @pl.when(e == 4)
         def _():
@@ -316,18 +320,15 @@
             @pl.when(home == 0)
             def _():
                 guest_load.wait()
-
-        @pl.when(e == 5)
+                owned_in(2).wait_recv()
+
+        @pl.when(e + 100 * (1 - home) * u == 4 * (1 - home))
+        def _():
+            both(1 - home, home * (2 - u) + (1 - home) * 2)
+
+        @pl.when(e == 6)
         def _():
             foreign_wait(6)
-
-        @pl.when((1 - home) * e == 2)
-        def _():
-            owned_in(1).wait_recv()
-
-        @pl.when((1 - home) * e == 8)
-        def _():
-            owned_in(2).wait_recv()
 
         def emit(i, rows, value):
             q, half, part = place(i)
@@ -335,23 +336,20 @@
 
         solve(a, b, emit)
 
-        @pl.when(e == 5)
+        @pl.when(e == 6)
         def _():
             twin_copy(0).start()
 
-        @pl.when(e == 6)
-        def _():
+        @pl.when(e == 7)
+        def _():
+            twin_copy(1).start()
             pass_on(0)
 
-        @pl.when(e == 7)
-        def _():
-            twin_copy(1).start()
-
         @pl.when(e == 8)
         def _():
             pass_on(1)
 
-        @pl.when(e == 9)
+        @pl.when(e == 10)
         def _():
             finish(0)
 

time: 103 us -> 98.4 us (0.955)
  Pallas kernels: 98.6 us -> 93.9 us
    pallas_call x1, Pallas kernels: 98.6 us -> 93.9 us  [body(): pl.pallas_call(fused_kernel, out_shape=jax.ShapeDtypeStruct((6, 512, NZ),...]
where the time goes in v6:
time: 98.4 us; the launch traced here: 96.6 us
  Pallas kernels  93.9 us (95%)
  local copies, waits for them, and re-layouts  2.73 us (3%)
    pallas_call x1, Pallas kernels, body(): pl.pallas_call(fused_kernel, out_shape=jax.ShapeDtypeStruct((6, 512, NZ),...  93.9 us
    unnamed x1, local copies, waits for them, and re-layouts  2.73 us

profile of v6, /device:TPU:6, one launch (start us, length us, event | category | flops | bytes accessed | tf_op | source)
XLA Modules:
  0.0 96.6 jit_solution(7982199603977050733)
XLA Ops:
  0.0 93.9 %shard_map.46 = f32[6,512,128]{2,1,0:T(8,128)} custom-call(f32[6,4096,128]{2,1,0:T(8,128)} %bitcast.3, f32[4096,128]{1,0:T(8,128)} %constant.8.clone.kernel_in, bf16[256,256]{1,0:T(8,128)(2,1)} %constant.6.clone.z_ref, bf16[256,256]{1,0:T(8,128)(2,1)} %constant.7.clone.r_ref), custom_call_target="tpu_custom_call" | custom-call | flops 65000001536 | bytes 30000000 | tf_op jit(solution)/shard_map/pallas_call | solution.py:399
  93.9 2.7 %copy.6 = f32[6,8,64,128]{3,2,1,0:T(8,128)} copy(f32[6,8,64,128]{3,2,1,0:T(8,128)} %bitcast.2) | data formatting | bytes 3145728

commit v7 on v6

--- a/solution.py
+++ b/solution.py
@@ -280,38 +280,36 @@
     def place(i):
         return i // 4, (i // 2) % 2, pl.ds(pl.multiple_of((i % 2) * 256, 256), 256)
 
-    def solve(a, b, emit):
-        forward(lambda rows: held[a, rows, :] * held[b, rows, :], table_z, table_r, first_ref)
-        middle(kernel_ref, table_r, first_ref, second_ref)
-        backward(emit, table_z, table_r, second_ref)
-
-    def both(a, b):
-        def emit(i, rows, value):
-            q, half, part = place(i)
-            sums[a, q, half, part, :] += held[b, rows, :] * value
-            sums[b, q, half, part, :] += held[a, rows, :] * value
-
-        solve(a, b, emit)
-
     for copy in loads:
         copy.wait()
 
-    def edge(e, _):
-        late, mid = e // 8, (e // 4) % 2
-        a = late * 2 + (1 - late) * ((1 - mid) * ((e // 2) % 2) + mid * (e % 2))
-        slot = 3 + late * (e % 4) + (1 - late) * ((1 - mid) * (e % 2) + mid * (2 + (e // 2) % 2))
+    mutual = (1 - home) * (4 + 8 * u)
+    idle = (1 - home) * u
+
+    def edge(t, _):
+        past = (t + 15 - mutual) // 16
+        now = (t + 16 - mutual) // 16 - past
+        e = t - past
+        from_4, from_6, from_7, from_9, from_10 = ((e + 16 - n) // 16 for n in (4, 6, 7, 9, 10))
+        a = (1 - from_4) * (e // 2) + (from_4 - from_10) * ((e + 2) % 3) + from_10 * 2
+        slot = (
+            (1 - from_4) * (3 + e % 2) + (from_4 - from_6) * 5 + (from_6 - from_7) * 3
+            + (from_7 - from_9) * 6 + from_9 * (e - 5)
+        )
         itself = home * u * ((7 - slot) // 3 - (6 - slot) // 3)
         b = slot + itself * (a - slot)
-
-        @pl.when((1 - home) * e == 2)
+        a = now * (1 - home) + (1 - now) * a
+        b = now * (2 - home * u) + (1 - now) * b
+
+        @pl.when((1 - home) * t == 2)
         def _():
             owned_in(1).wait_recv()
 
-        @pl.when(e == 3)
+        @pl.when(t == 3 + home)
         def _():
             foreign_in(1).start()
 
-        @pl.when(e == 4)
+        @pl.when(t == 4 + home)
         def _():
             @pl.when(home == 1)
             def _():
@@ -322,44 +320,53 @@
                 guest_load.wait()
                 owned_in(2).wait_recv()
 
-        @pl.when(e + 100 * (1 - home) * u == 4 * (1 - home))
-        def _():
-            both(1 - home, home * (2 - u) + (1 - home) * 2)
-
-        @pl.when(e == 6)
+        @pl.when(e == 7)
         def _():
             foreign_wait(6)
 
-        def emit(i, rows, value):
-            q, half, part = place(i)
-            sums[a, q, half, part, :] += held[b, rows, :] * value
-
-        solve(a, b, emit)
-
-        @pl.when(e == 6)
+        @pl.when(idle * t != 12)
+        def _():
+            forward(lambda rows: held[a, rows, :] * held[b, rows, :], table_z, table_r, first_ref)
+            middle(kernel_ref, table_r, first_ref, second_ref)
+
+            @pl.when(now == 0)
+            def _():
+                def emit(i, rows, value):
+                    q, half, part = place(i)
+                    sums[a, q, half, part, :] += held[b, rows, :] * value
+
+                backward(emit, table_z, table_r, second_ref)
+
+            @pl.when(now == 1)
+            def _():
+                def emit(i, rows, value):
+                    q, half, part = place(i)
+                    sums[a, q, half, part, :] += held[b, rows, :] * value
+                    sums[b, q, half, part, :] += held[a, rows, :] * value
+
+                backward(emit, table_z, table_r, second_ref)
+
+        @pl.when(e == 7)
         def _():
             twin_copy(0).start()
 
-        @pl.when(e == 7)
+        @pl.when(e == 8)
         def _():
             twin_copy(1).start()
             pass_on(0)
 
-        @pl.when(e == 8)
+        @pl.when(e == 9)
         def _():
             pass_on(1)
 
-        @pl.when(e == 10)
-        def _():
+        @pl.when(e == 11)
+        def _():
+            twin_copy(2).start()
             finish(0)
 
-        @pl.when(e == 11)
-        def _():
-            twin_copy(2).start()
-
         return 0
 
-    lax.fori_loop(0, 12, edge, 0)
+    lax.fori_loop(0, 13, edge, 0)
     pass_on(2)
     finish(1)
     finish(2)

time: 98.4 us -> 100 us (1.016)
  the two profiles are of different devices: /device:TPU:6 before, /device:TPU:8 now
where the time goes in v7:
time: 100 us
  Pallas kernels  97.5 us (98%)
  local copies, waits for them, and re-layouts  2.73 us (3%)
    pallas_call x1, Pallas kernels, body(): pl.pallas_call(fused_kernel, out_shape=jax.ShapeDtypeStruct((6, 512, NZ),...  97.5 us
    unnamed x1, local copies, waits for them, and re-layouts  2.73 us

profile of v7, /device:TPU:8, one launch (start us, length us, event | category | flops | bytes accessed | tf_op | source)
XLA Modules:
  0.0 100.2 jit_solution(6381574989005263402)
XLA Ops:
  0.0 97.5 %shard_map.46 = f32[6,512,128]{2,1,0:T(8,128)} custom-call(f32[6,4096,128]{2,1,0:T(8,128)} %bitcast.3, f32[4096,128]{1,0:T(8,128)} %constant.8.clone.kernel_in, bf16[256,256]{1,0:T(8,128)(2,1)} %constant.6.clone.z_ref, bf16[256,256]{1,0:T(8,128)(2,1)} %constant.7.clone.r_ref), custom_call_target="tpu_custom_call" | custom-call | flops 65000001536 | bytes 30000000 | tf_op jit(solution)/shard_map/pallas_call | solution.py:406
  97.5 2.7 %copy.6 = f32[6,8,64,128]{3,2,1,0:T(8,128)} copy(f32[6,8,64,128]{3,2,1,0:T(8,128)} %bitcast.2) | data formatting | bytes 3145728

commit v8 on v7

--- a/solution.py
+++ b/solution.py
@@ -237,8 +237,16 @@
 
     table_load.wait()
 
-    def twin_copy(v):
-        return remote(sums.at[v, :, 1 - keep], twin_part.at[v], twin_send.at[v], twin_recv.at[v], twin_id)
+    slabs = (3 - near_y, near_y, far_y, y)
+
+    def twin_copy(v, k):
+        row, index = slabs[k], 4 * v + k
+        source, target_ref = sums.at[v, row, 1 - keep], twin_part.at[v, row]
+        return remote(source, target_ref, twin_send.at[index], twin_recv.at[index], twin_id)
+
+    def twin_start(v):
+        for k in range(4):
+            twin_copy(v, k).start()
 
     def side_copy(v, k):
         row = (near_y, 3 - near_y)[k]
@@ -256,13 +264,14 @@
         return pltpu.make_async_copy(sums.at[v, y, keep], out_ref.at[3 * h + v], out_sem.at[v])
 
     def pass_on(v):
-        twin_copy(v).wait_recv()
-        for k, row in ((1, 3 - near_y), (0, near_y)):
-            sums[v, row, keep] += twin_part[v, row]
-            side_copy(v, k).start()
+        for k in range(2):
+            twin_copy(v, k).wait_recv()
+            sums[v, slabs[k], keep] += twin_part[v, slabs[k]]
+            side_copy(v, 1 - k).start()
 
     def finish(v):
         for k, row in ((1, far_y), (0, y)):
+            twin_copy(v, 3 - k).wait_recv()
             side_copy(v, k).wait_recv()
             sums[v, row, keep] += twin_part[v, row] + side_part[v, k]
             if k == 1:
@@ -290,12 +299,9 @@
         past = (t + 15 - mutual) // 16
         now = (t + 16 - mutual) // 16 - past
         e = t - past
-        from_4, from_6, from_7, from_9, from_10 = ((e + 16 - n) // 16 for n in (4, 6, 7, 9, 10))
-        a = (1 - from_4) * (e // 2) + (from_4 - from_10) * ((e + 2) % 3) + from_10 * 2
-        slot = (
-            (1 - from_4) * (3 + e % 2) + (from_4 - from_6) * 5 + (from_6 - from_7) * 3
-            + (from_7 - from_9) * 6 + from_9 * (e - 5)
-        )
+        late, mid = e // 8, (e // 4) % 2
+        a = late * 2 + (1 - late) * ((1 - mid) * ((e // 2) % 2) + mid * (e % 2))
+        slot = 3 + late * (e % 4) + (1 - late) * ((1 - mid) * (e % 2) + mid * (2 + (e // 2) % 2))
         itself = home * u * ((7 - slot) // 3 - (6 - slot) // 3)
         b = slot + itself * (a - slot)
         a = now * (1 - home) + (1 - now) * a
@@ -320,7 +326,7 @@
                 guest_load.wait()
                 owned_in(2).wait_recv()
 
-        @pl.when(e == 7)
+        @pl.when(e == 6)
         def _():
             foreign_wait(6)
 
@@ -328,6 +334,14 @@
         def _():
             forward(lambda rows: held[a, rows, :] * held[b, rows, :], table_z, table_r, first_ref)
             middle(kernel_ref, table_r, first_ref, second_ref)
+
+            @pl.when(e == 7)
+            def _():
+                pass_on(0)
+
+            @pl.when(e == 8)
+            def _():
+                pass_on(1)
 
             @pl.when(now == 0)
             def _():
@@ -346,23 +360,21 @@
 
                 backward(emit, table_z, table_r, second_ref)
 
+        @pl.when(e == 6)
+        def _():
+            twin_start(0)
+
         @pl.when(e == 7)
         def _():
-            twin_copy(0).start()
-
-        @pl.when(e == 8)
-        def _():
-            twin_copy(1).start()
-            pass_on(0)
-
-        @pl.when(e == 9)
-        def _():
-            pass_on(1)
+            twin_start(1)
+
+        @pl.when(e == 10)
+        def _():
+            finish(0)
 
         @pl.when(e == 11)
         def _():
-            twin_copy(2).start()
-            finish(0)
+            twin_start(2)
 
         return 0
 
@@ -388,7 +400,8 @@
 
     for v in range(3):
         foreign_in(v).wait_send()
-        twin_copy(v).wait_send()
+        for k in range(4):
+            twin_copy(v, k).wait_send()
         side_copy(v, 0).wait_send()
         side_copy(v, 1).wait_send()
         out_copy(v, 1).wait_send()
@@ -417,7 +430,7 @@
             buffer(3, 4, 512, NZ),
             buffer(3, 2, 512, NZ),
         ]
-        + [pltpu.SemaphoreType.DMA((count,)) for count in (7, 3, 3, 3, 4, 3, 3, 6, 6, 6, 6, 3)],
+        + [pltpu.SemaphoreType.DMA((count,)) for count in (7, 3, 3, 3, 4, 12, 12, 6, 6, 6, 6, 3)],
         compiler_params=pltpu.CompilerParams(
             vmem_limit_bytes=VMEM_LIMIT, collective_id=0, has_side_effects=True
         ),

time: 100 us -> 96.8 us (0.968)
  the two profiles are of different devices: /device:TPU:8 before, /device:TPU:6 now
where the time goes in v8:
time: 96.8 us; the launch traced here: 95.5 us
  Pallas kernels  92.7 us (96%)
  local copies, waits for them, and re-layouts  2.73 us (3%)
    pallas_call x1, Pallas kernels, body(): pl.pallas_call(fused_kernel, out_shape=jax.ShapeDtypeStruct((6, 512, NZ),...  92.7 us
    unnamed x1, local copies, waits for them, and re-layouts  2.73 us

profile of v8, /device:TPU:6, one launch (start us, length us, event | category | flops | bytes accessed | tf_op | source)
XLA Modules:
  0.0 95.5 jit_solution(8699420970025671800)
XLA Ops:
  0.0 92.7 %shard_map.46 = f32[6,512,128]{2,1,0:T(8,128)} custom-call(f32[6,4096,128]{2,1,0:T(8,128)} %bitcast.3, f32[4096,128]{1,0:T(8,128)} %constant.8.clone.kernel_in, bf16[256,256]{1,0:T(8,128)(2,1)} %constant.6.clone.z_ref, bf16[256,256]{1,0:T(8,128)(2,1)} %constant.7.clone.r_ref), custom_call_target="tpu_custom_call" | custom-call | flops 65000001536 | bytes 30000000 | tf_op jit(solution)/shard_map/pallas_call | solution.py:419
  92.7 2.7 %copy.6 = f32[6,8,64,128]{3,2,1,0:T(8,128)} copy(f32[6,8,64,128]{3,2,1,0:T(8,128)} %bitcast.2) | data formatting | bytes 3145728

commit v9 on v8

--- a/solution.py
+++ b/solution.py
@@ -216,8 +216,7 @@
 
     @pl.when(home == 1)
     def _():
-        for v in range(3):
-            owned_in(v).start()
+        owned_in(0).start()
 
     for j in (0, 2):
         foreign_in(j).start()
@@ -306,6 +305,11 @@
         b = slot + itself * (a - slot)
         a = now * (1 - home) + (1 - now) * a
         b = now * (2 - home * u) + (1 - now) * b
+
+        @pl.when(home * t == 1)
+        def _():
+            owned_in(1).start()
+            owned_in(2).start()
 
         @pl.when((1 - home) * t == 2)
         def _():

time: 96.8 us -> 97.1 us (level)
  no operation moved by 1% of the time
where the time goes in v9:
time: 97.1 us; the launch traced here: 95.7 us
  Pallas kernels  92.9 us (96%)
  local copies, waits for them, and re-layouts  2.73 us (3%)
    pallas_call x1, Pallas kernels, body(): pl.pallas_call(fused_kernel, out_shape=jax.ShapeDtypeStruct((6, 512, NZ),...  92.9 us
    unnamed x1, local copies, waits for them, and re-layouts  2.73 us

profile of v9, /device:TPU:6, one launch (start us, length us, event | category | flops | bytes accessed | tf_op | source)
XLA Modules:
  0.0 95.7 jit_solution(11809213096663622021)
XLA Ops:
  0.0 92.9 %shard_map.46 = f32[6,512,128]{2,1,0:T(8,128)} custom-call(f32[6,4096,128]{2,1,0:T(8,128)} %bitcast.3, f32[4096,128]{1,0:T(8,128)} %constant.8.clone.kernel_in, bf16[256,256]{1,0:T(8,128)(2,1)} %constant.6.clone.z_ref, bf16[256,256]{1,0:T(8,128)(2,1)} %constant.7.clone.r_ref), custom_call_target="tpu_custom_call" | custom-call | flops 65000001536 | bytes 30000000 | tf_op jit(solution)/shard_map/pallas_call | solution.py:423
  93.0 2.7 %copy.6 = f32[6,8,64,128]{3,2,1,0:T(8,128)} copy(f32[6,8,64,128]{3,2,1,0:T(8,128)} %bitcast.2) | data formatting | bytes 3145728

commit v10 on v9

--- a/solution.py
+++ b/solution.py
@@ -315,7 +315,7 @@
         def _():
             owned_in(1).wait_recv()
 
-        @pl.when(t == 3 + home)
+        @pl.when(t == 2 + home)
         def _():
             foreign_in(1).start()
 

time: 97.1 us -> 97.1 us (level)
  no operation moved by 1% of the time
where the time goes in v10:
time: 97.1 us; the launch traced here: 95.7 us
  Pallas kernels  92.9 us (96%)
  local copies, waits for them, and re-layouts  2.73 us (3%)
    pallas_call x1, Pallas kernels, body(): pl.pallas_call(fused_kernel, out_shape=jax.ShapeDtypeStruct((6, 512, NZ),...  92.9 us
    unnamed x1, local copies, waits for them, and re-layouts  2.73 us

profile of v10, /device:TPU:6, one launch (start us, length us, event | category | flops | bytes accessed | tf_op | source)
XLA Modules:
  0.0 95.7 jit_solution(11834490402201027372)
XLA Ops:
  0.0 92.9 %shard_map.46 = f32[6,512,128]{2,1,0:T(8,128)} custom-call(f32[6,4096,128]{2,1,0:T(8,128)} %bitcast.3, f32[4096,128]{1,0:T(8,128)} %constant.8.clone.kernel_in, bf16[256,256]{1,0:T(8,128)(2,1)} %constant.6.clone.z_ref, bf16[256,256]{1,0:T(8,128)(2,1)} %constant.7.clone.r_ref), custom_call_target="tpu_custom_call" | custom-call | flops 65000001536 | bytes 30000000 | tf_op jit(solution)/shard_map/pallas_call | solution.py:423
  93.0 2.7 %copy.6 = f32[6,8,64,128]{3,2,1,0:T(8,128)} copy(f32[6,8,64,128]{3,2,1,0:T(8,128)} %bitcast.2) | data formatting | bytes 3145728

commit v11 on v8

--- a/solution.py
+++ b/solution.py
@@ -289,9 +289,6 @@
     def place(i):
         return i // 4, (i // 2) % 2, pl.ds(pl.multiple_of((i % 2) * 256, 256), 256)
 
-    for copy in loads:
-        copy.wait()
-
     mutual = (1 - home) * (4 + 8 * u)
     idle = (1 - home) * u
 
@@ -306,6 +303,14 @@
         b = slot + itself * (a - slot)
         a = now * (1 - home) + (1 - now) * a
         b = now * (2 - home * u) + (1 - now) * b
+
+        @pl.when(t == home)
+        def _():
+            loads[0].wait()
+
+        @pl.when(t == 1 + home)
+        def _():
+            loads[1].wait()
 
         @pl.when((1 - home) * t == 2)
         def _():

time: 96.8 us -> 96.8 us (level)
  no operation moved by 1% of the time
where the time goes in v11:
time: 96.8 us; the launch traced here: 95.5 us
  Pallas kernels  92.8 us (96%)
  local copies, waits for them, and re-layouts  2.73 us (3%)
    pallas_call x1, Pallas kernels, body(): pl.pallas_call(fused_kernel, out_shape=jax.ShapeDtypeStruct((6, 512, NZ),...  92.8 us
    unnamed x1, local copies, waits for them, and re-layouts  2.73 us

profile of v11, /device:TPU:6, one launch (start us, length us, event | category | flops | bytes accessed | tf_op | source)
XLA Modules:
  0.0 95.5 jit_solution(13710207450720732511)
XLA Ops:
  0.0 92.8 %shard_map.46 = f32[6,512,128]{2,1,0:T(8,128)} custom-call(f32[6,4096,128]{2,1,0:T(8,128)} %bitcast.3, f32[4096,128]{1,0:T(8,128)} %constant.8.clone.kernel_in, bf16[256,256]{1,0:T(8,128)(2,1)} %constant.6.clone.z_ref, bf16[256,256]{1,0:T(8,128)(2,1)} %constant.7.clone.r_ref), custom_call_target="tpu_custom_call" | custom-call | flops 65000001536 | bytes 30000000 | tf_op jit(solution)/shard_map/pallas_call | solution.py:424
  92.8 2.7 %copy.6 = f32[6,8,64,128]{3,2,1,0:T(8,128)} copy(f32[6,8,64,128]{3,2,1,0:T(8,128)} %bitcast.2) | data formatting | bytes 3145728
